TPU v7x, 128 devices: a whole 4x4x4 slice. The times are simulated.
128 devices in a mesh: clip: 4 (over y), tm: 4 (over z), space: 8 (over x, core).
Axes of the slice: x: 4, y: 4, z: 4, core: 2. Of those that a mesh axis runs over, the one named last changes fastest.
Arguments:
- latents: bfloat16 [8, 8, 16, 64, 384], P('clip', 'tm', 'space'), parts along dimension 0, may hold values from -6 to 6
- frame_counts: int32 [8], P('clip'), parts along dimension 0, may hold values from 1 to 8, as said below
- norm_gain: float32 [384], replicated, may hold values from 0.1 to 1.9
- norm_bias: float32 [384], replicated, may hold values from -3 to 3
- conv3_weight: bfloat16 [3, 3, 3, 384, 384], replicated, may hold values from -0.0625 to 0.0625
- conv3_bias: float32 [384], replicated, may hold values from -3 to 3
- conv2_weight: bfloat16 [3, 3, 384, 384], replicated, may hold values from -0.109375 to 0.109375
- conv2_bias: float32 [384], replicated, may hold values from -3 to 3
Outputs:
- decoded: bfloat16 [8, 8, 32, 128, 384], P('clip', 'tm', 'space'), parts along dimension 0
There are 4 independent parts, one for each index of `clip`. A program takes and returns all parts, laid end to end along the dimension named above; an argument that names none is the same for every part. Nothing has to cross between parts.
Inputs may be any that keep to these rules, and one draw needn't show every extreme that they name: `frame_counts`: each clip has between 1 and 8 real frames; in every draw some clip has all 8.
All inputs are finite; a program needn't handle non-finite values.
Results may differ from a plain program's by a relative error of at most 0.0051.
Values may be sent and summed in bfloat16 or wider, within the bound.
A program may use at most 64 MiB of HBM per device.

v0:
```python
import functools

import jax
import jax.numpy as jnp
from jax import lax
from jax.experimental import pallas as pl
from jax.experimental.pallas import tpu as pltpu
from jax.sharding import PartitionSpec as P

MESH = pl.DeviceIdType.MESH
EPS = 1e-05
CH = 384
GROUP = 12
COLS = 64
F32 = jnp.float32
BF16 = jnp.bfloat16
UNITS = ((0, 1), (0, 0), (1, 1), (1, 0))


def dot(a, b):
    return jnp.dot(a, b, preferred_element_type=F32)


def exact_dot(a, b):
    return jnp.dot(a, b, preferred_element_type=F32, precision=lax.Precision.HIGHEST)


def kernel(
    cells, lat, counts, gain, nbias, w3, b3, w2, b2, out,
    x, act, wide, raw2, phase, acc, mid, gath_t, gath_s, inter, coef,
    lsem, wsem, w2sem, ts_s, ts_r, ss_s, ss_r, z_s, z_r, h_s, h_r, c_s, c_r, m_s, m_r,
):
    n_t, n_s = lax.axis_size("tm"), lax.axis_size("space")
    t_me, s_me = lax.axis_index("tm"), lax.axis_index("space")
    along_t = lambda d: {"tm": lax.rem(t_me + d, n_t)}
    along_s = lambda d: {"space": lax.rem(s_me + d, n_s)}
    up, down = along_s(n_s - 1), along_s(1)

    def remote(src, dst, send, recv, device):
        return pltpu.make_async_remote_copy(
            src_ref=src, dst_ref=dst, send_sem=send, recv_sem=recv, device_id=device, device_id_type=MESH
        )

    own = pltpu.make_async_copy(lat, x.at[:, pl.ds(2, 2), pl.ds(1, 2)], lsem)
    own.start()
    w2_copy = pltpu.make_async_copy(w2, raw2, w2sem)
    w2_copy.start()
    w3_copies = [
        pltpu.make_async_copy(w3.at[a, :, e], wide.at[a, :, :, pl.ds(e * CH, CH)], wsem.at[a * 3 + e])
        for a in (2, 1, 0)
        for e in range(3)
    ]
    for copy in w3_copies:
        copy.start()

    barrier = pltpu.get_barrier_semaphore()
    peers = [along_t(d) for d in range(1, n_t)] + [along_s(d) for d in range(1, n_s)]
    for peer in peers:
        pl.semaphore_signal(barrier, inc=1, device_id=peer, device_id_type=MESH)

    def present(c, frame):
        return (frame < counts[c]).astype(F32)

    own.wait()
    firsts, seconds = [], []
    for c in range(2):
        first = jnp.zeros((8, CH), F32)
        second = jnp.zeros((8, CH), F32)
        for f in range(2):
            f1 = jnp.zeros((8, CH), F32)
            f2 = jnp.zeros((8, CH), F32)
            for r in range(2):
                v = x[c, 2 + f, 1 + r].astype(F32).reshape(8, 8, CH)
                f1 += jnp.sum(v, axis=0)
                f2 += jnp.sum(v * v, axis=0)
            there = present(c, 2 * t_me + f)
            first += f1 * there
            second += f2 * there
        firsts.append(jnp.sum(first, axis=0, keepdims=True))
        seconds.append(jnp.sum(second, axis=0, keepdims=True))
    sums = jnp.concatenate(firsts + seconds + [jnp.zeros((4, CH), F32)], axis=0)
    channel = lax.broadcasted_iota(jnp.int32, (CH, 128), 0)
    low = lax.broadcasted_iota(jnp.int32, (CH, 128), 1) * GROUP
    member = jnp.where((channel >= low) & (channel < low + GROUP), 1.0, 0.0).astype(F32)
    gath_t[0] = exact_dot(sums, member)

    pl.semaphore_wait(barrier, len(peers))

    stat_t = [remote(gath_t.at[0], gath_t.at[d], ts_s.at[d], ts_r.at[d], along_t(d)) for d in range(1, n_t)]
    for copy in stat_t:
        copy.start()
    z_copies = {
        (c, f): remote(lat.at[c, f], x.at[c, f, pl.ds(1, 2)], z_s.at[c * 2 + f], z_r.at[c * 2 + f], along_t(1))
        for c, f in UNITS
    }

    @pl.when(t_me < n_t - 1)
    def _():
        for unit in UNITS:
            z_copies[unit].start()

    halo = []
    for c in range(2):
        halo.append((
            remote(lat.at[c, :, 1], x.at[c, pl.ds(2, 2), 0], h_s.at[2 * c], h_r.at[2 * c], down),
            remote(lat.at[c, :, 0], x.at[c, pl.ds(2, 2), 3], h_s.at[2 * c + 1], h_r.at[2 * c + 1], up),
        ))
    for pair in halo:
        for copy in pair:
            copy.start()

    w2_copy.wait()

    def fold(i, carry):
        rows = pl.ds(pl.multiple_of(i * 64, 64), 64)
        by_row = [[raw2[b, e, rows].astype(F32) for e in range(3)] for b in range(3)]
        for p, u, picks in ((0, 0, (0,)), (0, 1, (1, 2)), (1, 0, (0, 1)), (1, 1, (2,))):
            taps = [functools.reduce(jnp.add, [by_row[b][e] for b in picks]) for e in range(3)]
            phase[p, u, rows, 0:CH] = taps[0].astype(BF16)
            phase[p, u, rows, CH : 2 * CH] = (taps[0] + taps[1] + taps[2]).astype(BF16)
            phase[p, u, rows, 2 * CH : 3 * CH] = taps[2].astype(BF16)
        return carry

    lax.fori_loop(0, CH // 64, fold, 0)

    for copy in stat_t:
        copy.wait_recv()
    gath_s[0] = gath_t[0] + gath_t[1] + gath_t[2] + gath_t[3]
    stat_s = [remote(gath_s.at[0], gath_s.at[d], ss_s.at[d], ss_r.at[d], along_s(d)) for d in range(1, n_s)]
    for copy in stat_s:
        copy.start()

    corner = {
        (c, f): (
            remote(x.at[c, f, 2], x.at[c, f, 0], c_s.at[c * 4 + f * 2], c_r.at[c * 4 + f * 2], down),
            remote(x.at[c, f, 1], x.at[c, f, 3], c_s.at[c * 4 + f * 2 + 1], c_r.at[c * 4 + f * 2 + 1], up),
        )
        for c, f in UNITS
    }

    def forward(unit):
        @pl.when(t_me > 0)
        def _():
            z_copies[unit].wait_recv()
            for copy in corner[unit]:
                copy.start()

    forward(UNITS[0])

    for copy in stat_s:
        copy.wait_recv()
    total = gath_s[0]
    for d in range(1, n_s):
        total = total + gath_s[d]
    means, scales = [], []
    for c in range(2):
        number = (counts[c] * (cells * GROUP)).astype(F32)
        mean = total[c : c + 1] / number
        variance = total[2 + c : 3 + c] / number - mean * mean
        means.append(mean)
        scales.append(lax.rsqrt(variance + EPS))
    packed = jnp.concatenate(means + scales + [jnp.zeros((4, 128), F32)], axis=0)
    group = lax.broadcasted_iota(jnp.int32, (128, CH), 0) * GROUP
    channel = lax.broadcasted_iota(jnp.int32, (128, CH), 1)
    spread = jnp.where((channel >= group) & (channel < group + GROUP), 1.0, 0.0).astype(F32)
    coef[...] = exact_dot(packed, spread)

    def activate(c, f):
        there = present(c, 2 * t_me - 2 + f)

        def row(r, carry):
            inside = jnp.where(((r == 0) & (s_me == 0)) | ((r == 3) & (s_me == n_s - 1)), 0.0, there)
            half = (x[c, f, r].astype(F32) - coef[c : c + 1]) * (coef[2 + c : 3 + c] * gain[...] * 0.5) + nbias[...] * 0.5
            act[c, f, r] = ((half + half * jnp.tanh(half)) * inside).astype(BF16)
            return carry

        lax.fori_loop(0, 4, row, 0)

    column = lax.rem(lax.broadcasted_iota(jnp.int32, (2 * COLS, CH), 0), COLS)
    not_first, not_last = column > 0, column < COLS - 1

    def before(v):
        return jnp.where(not_first, pltpu.roll(v, 1, 0), 0.0)

    def after(v):
        return jnp.where(not_last, pltpu.roll(v, 2 * COLS - 1, 0), 0.0)

    def volume(c, frames, taps):
        lhs = jnp.concatenate(
            [jnp.concatenate([act[c, f, r + b] for f in frames for b in range(3)], axis=1) for r in range(2)], axis=0
        )
        rhs = wide[pl.ds(taps[0], len(taps))].reshape(len(taps) * 3 * CH, 3 * CH)
        prod = dot(lhs, rhs)
        return before(prod[:, 0:CH]) + prod[:, CH : 2 * CH] + after(prod[:, 2 * CH :])

    def own_part(c):
        acc[c, 0] = volume(c, (2,), (2,))
        acc[c, 1] = volume(c, (2, 3), (1, 2))

    def finish(c):
        for f in range(2):
            kept = present(c, 2 * t_me + f)
            resid = jnp.concatenate([x[c, 2 + f, 1], x[c, 2 + f, 2]], axis=0).astype(F32)
            value = ((resid + acc[c, f] + b3[...]) * kept).astype(BF16)
            mid[c, f, 1] = value[:COLS]
            mid[c, f, 2] = value[COLS:]

    mid_copies = [
        (
            remote(mid.at[c, :, 2], mid.at[c, :, 0], m_s.at[2 * c], m_r.at[2 * c], down),
            remote(mid.at[c, :, 1], mid.at[c, :, 3], m_s.at[2 * c + 1], m_r.at[2 * c + 1], up),
        )
        for c in range(2)
    ]

    def emit(c, p, r, first_row):
        lhs = jnp.concatenate([jnp.concatenate([mid[c, f, first_row], mid[c, f, first_row + 1]], axis=1) for f in range(2)], axis=0)
        prod = dot(lhs, phase[p].reshape(2 * CH, 3 * CH))
        left, centre, right = prod[:, 0:CH], prod[:, CH : 2 * CH], prod[:, 2 * CH :]
        centre = centre + b2[...]
        even = centre + (before(left) - left)
        odd = centre + (after(right) - right)
        for f in range(2):
            kept = present(c, 2 * t_me + f)
            for lane in range(CH // 128):
                cut = slice(lane * 128, lane * 128 + 128)
                rows = slice(f * COLS, (f + 1) * COLS)
                inter[f, lane, pl.ds(0, COLS, stride=2)] = even[rows, cut] * kept
                inter[f, lane, pl.ds(1, COLS, stride=2)] = odd[rows, cut] * kept
                out[c, f, 2 * r + p, :, cut] = inter[f, lane].astype(BF16)

    def inner(c):
        emit(c, 1, 0, 1)
        emit(c, 0, 1, 1)

    def outer(c):
        for copy in mid_copies[c]:
            copy.wait_recv()

        @pl.when(s_me == 0)
        def _():
            mid[c, :, 0] = jnp.zeros((2, COLS, CH), BF16)

        @pl.when(s_me == n_s - 1)
        def _():
            mid[c, :, 3] = jnp.zeros((2, COLS, CH), BF16)

        emit(c, 0, 0, 0)
        emit(c, 1, 1, 2)

    def arrived(unit):
        for copy in corner[unit]:
            copy.wait_recv()

    for copy in halo[0]:
        copy.wait_recv()
    activate(0, 2)
    activate(0, 3)
    forward(UNITS[1])
    for copy in w3_copies:
        copy.wait()
    own_part(0)
    for copy in halo[1]:
        copy.wait_recv()
    activate(1, 2)
    activate(1, 3)
    forward(UNITS[2])
    own_part(1)
    forward(UNITS[3])

    @pl.when(t_me > 0)
    def _():
        arrived((0, 1))
        activate(0, 1)
        arrived((0, 0))
        activate(0, 0)
        acc[0, 1] += volume(0, (1,), (0,))
        acc[0, 0] += volume(0, (0, 1), (0, 1))

    finish(0)
    for copy in mid_copies[0]:
        copy.start()

    @pl.when(t_me > 0)
    def _():
        arrived((1, 1))
        activate(1, 1)
        acc[1, 1] += volume(1, (1,), (0,))
        acc[1, 0] += volume(1, (1,), (1,))
        arrived((1, 0))
        activate(1, 0)
        acc[1, 0] += volume(1, (0,), (0,))

    finish(1)
    for copy in mid_copies[1]:
        copy.start()

    inner(0)
    outer(0)
    inner(1)
    outer(1)

    for copy in stat_t + stat_s + [copy for pair in halo + mid_copies for copy in pair]:
        copy.wait_send()

    @pl.when(t_me < n_t - 1)
    def _():
        for unit in UNITS:
            z_copies[unit].wait_send()

    @pl.when(t_me > 0)
    def _():
        for unit in UNITS:
            for copy in corner[unit]:
                copy.wait_send()


def body(latents, frame_counts, norm_gain, norm_bias, conv3_weight, conv3_bias, conv2_weight, conv2_bias):
    rows = latents.shape[2] * lax.axis_size("space")
    row = lambda v: v.reshape(1, CH)
    hbm, vmem, smem = (pl.BlockSpec(memory_space=space) for space in (pl.ANY, pltpu.VMEM, pltpu.SMEM))
    dma = pltpu.SemaphoreType.DMA
    return pl.pallas_call(
        functools.partial(kernel, rows * COLS),
        out_shape=jax.ShapeDtypeStruct((2, 2, 4, 2 * COLS, CH), BF16),
        in_specs=[hbm, smem, vmem, vmem, hbm, vmem, hbm, vmem],
        out_specs=vmem,
        scratch_shapes=[
            pltpu.VMEM((2, 4, 4, COLS, CH), BF16),
            pltpu.VMEM((2, 4, 4, COLS, CH), BF16),
            pltpu.VMEM((3, 3, CH, 3 * CH), BF16),
            pltpu.VMEM((3, 3, CH, CH), BF16),
            pltpu.VMEM((2, 2, CH, 3 * CH), BF16),
            pltpu.VMEM((2, 2, 2 * COLS, CH), F32),
            pltpu.VMEM((2, 2, 4, COLS, CH), BF16),
            pltpu.VMEM((4, 8, 128), F32),
            pltpu.VMEM((8, 8, 128), F32),
            pltpu.VMEM((2, 3, 2 * COLS, 128), F32),
            pltpu.VMEM((8, CH), F32),
            dma, dma((9,)), dma, dma((4,)), dma((4,)), dma((8,)), dma((8,)),
            dma((4,)), dma((4,)), dma((4,)), dma((4,)), dma((8,)), dma((8,)), dma((4,)), dma((4,)),
        ],
        compiler_params=pltpu.CompilerParams(collective_id=0, has_side_effects=True, vmem_limit_bytes=58 * 2**20),
        cost_estimate=pl.CostEstimate(flops=7 * 10**9, bytes_accessed=13 * 10**6, transcendentals=10**6),
    )(latents, frame_counts, row(norm_gain), row(norm_bias), conv3_weight, row(conv3_bias), conv2_weight, row(conv2_bias))


def solution(mesh):
    placed = (P("clip", "tm", "space", None, None), P("clip"), P(), P(), P(), P(), P(), P())
    return jax.shard_map(
        body, mesh=mesh, in_specs=placed, out_specs=P("clip", "tm", "space", None, None), check_vma=False
    )
```

profile of v0, /device:TPU:40, one launch (start us, length us, event | category | flops | bytes accessed | tf_op | source)
XLA Modules:
  0.0 33.4 jit_solution(520577176969649840)
XLA Ops:
  0.0 1.2 %reshape.12.gain = f32[1,384]{1,0:T(1,128)} reshape(f32[384]{0:T(512)} %param.10) | data formatting | bytes 3072 | tf_op jit(solution)/shard_map/reshape | solution.py:320
  1.2 1.3 %reshape.13.nbias = f32[1,384]{1,0:T(1,128)} reshape(f32[384]{0:T(512)} %param.11) | data formatting | bytes 3072 | tf_op jit(solution)/shard_map/reshape | solution.py:320
  2.5 1.3 %reshape.14.b3 = f32[1,384]{1,0:T(1,128)} reshape(f32[384]{0:T(512)} %param.13) | data formatting | bytes 3072 | tf_op jit(solution)/shard_map/reshape | solution.py:320
  3.8 1.2 %reshape.15.b2 = f32[1,384]{1,0:T(1,128)} reshape(f32[384]{0:T(512)} %param.15) | data formatting | bytes 3072 | tf_op jit(solution)/shard_map/reshape | solution.py:320
  5.0 25.7 %shard_map.82 = bf16[2,2,4,128,384]{4,3,2,1,0:T(8,128)(2,1)} custom-call(bf16[2,2,2,64,384]{4,3,2,1,0:T(8,128)(2,1)} %lat.1, s32[2]{0:T(128)} %counts.1, f32[1,384]{1,0:T(1,128)} %reshape.12.gain, f32[1,384]{1,0:T(1,128)} %reshape.13.nbias, bf16[3,3,3,384,384]{4,3,2,1,0:T(8,128)(2,1)} %w3.1, f32[1,384]{1,0:T(1,128)} %reshape.14.b3, ...), custom_call_target="tpu_custom_call" | custom-call | flops 7000000000 | bytes 13000000 | tf_op jit(solution)/shard_map/pallas_call | solution.py:323
  30.7 2.8 %copy.10 = bf16[2,2,4,128,384]{4,3,2,1,0:T(8,128)(2,1)} copy(bf16[2,2,4,128,384]{4,3,2,1,0:T(8,128)(2,1)} %shard_map.82) | data formatting | bytes 3145728
where the time goes:
time: 33.7 us; the launch traced here: 33.4 us
  Pallas kernels  25.7 us (76%)
  local copies, waits for them, and re-layouts  7.76 us (23%)
    pallas_call x1, Pallas kernels, body(): pl.pallas_call(functools.partial(kernel, rows * COLS), out_shape=jax.Shap...  25.7 us
    reshape x4, local copies, waits for them, and re-layouts, body(): row = lambda v: v.reshape(1, CH)  5 us
    unnamed x1, local copies, waits for them, and re-layouts  2.76 us

commit v1 on v0

--- a/solution.py
+++ b/solution.py
@@ -170,7 +170,7 @@
 
         def row(r, carry):
             inside = jnp.where(((r == 0) & (s_me == 0)) | ((r == 3) & (s_me == n_s - 1)), 0.0, there)
-            half = (x[c, f, r].astype(F32) - coef[c : c + 1]) * (coef[2 + c : 3 + c] * gain[...] * 0.5) + nbias[...] * 0.5
+            half = (x[c, f, r].astype(F32) - coef[c : c + 1]) * (coef[2 + c : 3 + c] * gain[...].reshape(1, CH) * 0.5) + nbias[...].reshape(1, CH) * 0.5
             act[c, f, r] = ((half + half * jnp.tanh(half)) * inside).astype(BF16)
             return carry
 
@@ -201,7 +201,7 @@
         for f in range(2):
             kept = present(c, 2 * t_me + f)
             resid = jnp.concatenate([x[c, 2 + f, 1], x[c, 2 + f, 2]], axis=0).astype(F32)
-            value = ((resid + acc[c, f] + b3[...]) * kept).astype(BF16)
+            value = ((resid + acc[c, f] + b3[...].reshape(1, CH)) * kept).astype(BF16)
             mid[c, f, 1] = value[:COLS]
             mid[c, f, 2] = value[COLS:]
 
@@ -217,7 +217,7 @@
         lhs = jnp.concatenate([jnp.concatenate([mid[c, f, first_row], mid[c, f, first_row + 1]], axis=1) for f in range(2)], axis=0)
         prod = dot(lhs, phase[p].reshape(2 * CH, 3 * CH))
         left, centre, right = prod[:, 0:CH], prod[:, CH : 2 * CH], prod[:, 2 * CH :]
-        centre = centre + b2[...]
+        centre = centre + b2[...].reshape(1, CH)
         even = centre + (before(left) - left)
         odd = centre + (after(right) - right)
         for f in range(2):
@@ -317,8 +317,7 @@
 
 def body(latents, frame_counts, norm_gain, norm_bias, conv3_weight, conv3_bias, conv2_weight, conv2_bias):
     rows = latents.shape[2] * lax.axis_size("space")
-    row = lambda v: v.reshape(1, CH)
-    hbm, vmem, smem = (pl.BlockSpec(memory_space=space) for space in (pl.ANY, pltpu.VMEM, pltpu.SMEM))
+    hbm, vmem, smem = (pl.BlockSpec(memory_space=space) for space in (pltpu.HBM, pltpu.VMEM, pltpu.SMEM))
     dma = pltpu.SemaphoreType.DMA
     return pl.pallas_call(
         functools.partial(kernel, rows * COLS),
@@ -342,7 +341,7 @@
         ],
         compiler_params=pltpu.CompilerParams(collective_id=0, has_side_effects=True, vmem_limit_bytes=58 * 2**20),
         cost_estimate=pl.CostEstimate(flops=7 * 10**9, bytes_accessed=13 * 10**6, transcendentals=10**6),
-    )(latents, frame_counts, row(norm_gain), row(norm_bias), conv3_weight, row(conv3_bias), conv2_weight, row(conv2_bias))
+    )(latents, frame_counts, norm_gain, norm_bias, conv3_weight, conv3_bias, conv2_weight, conv2_bias)
 
 
 def solution(mesh):

time: 33.7 us -> 28.6 us (0.85)
  local copies, waits for them, and re-layouts: 7.76 us -> 2.76 us
    reshape x4 -> x0, local copies, waits for them, and re-layouts: 5 us -> none  [body(): row = lambda v: v.reshape(1, CH)]
where the time goes in v1:
time: 28.6 us; the launch traced here: 28.4 us
  Pallas kernels  25.7 us (90%)
  local copies, waits for them, and re-layouts  2.76 us (10%)
    pallas_call x1, Pallas kernels, body(): pl.pallas_call(functools.partial(kernel, rows * COLS), out_shape=jax.Shap...  25.7 us
    unnamed x1, local copies, waits for them, and re-layouts  2.76 us

profile of v1, /device:TPU:40, one launch (start us, length us, event | category | flops | bytes accessed | tf_op | source)
XLA Modules:
  0.0 28.4 jit_solution(1782078579271789530)
XLA Ops:
  0.0 25.7 %shard_map.82 = bf16[2,2,4,128,384]{4,3,2,1,0:T(8,128)(2,1)} custom-call(bf16[2,2,2,64,384]{4,3,2,1,0:T(8,128)(2,1)} %lat.1, s32[2]{0:T(128)} %counts.1, f32[384]{0:T(512)} %gain.1, f32[384]{0:T(512)} %nbias.1, bf16[3,3,3,384,384]{4,3,2,1,0:T(8,128)(2,1)} %w3.1, f32[384]{0:T(512)} %b3.1, bf16[3,3,384,384]{3,2,1,0:T(8,128)(2,1)} %w2.1, f32[384]{0:T(512)} %b2.1), custom_call_target="tpu_custom_call" | custom-call | flops 7000000000 | bytes 13000000 | tf_op jit(solution)/shard_map/pallas_call | solution.py:322
  25.7 2.8 %copy.10 = bf16[2,2,4,128,384]{4,3,2,1,0:T(8,128)(2,1)} copy(bf16[2,2,4,128,384]{4,3,2,1,0:T(8,128)(2,1)} %shard_map.82) | data formatting | bytes 3145728

commit v2 on v1

v2 whole, which is shorter than its diff:
```python
import functools

import jax
import jax.numpy as jnp
from jax import lax
from jax.experimental import pallas as pl
from jax.experimental.pallas import tpu as pltpu
from jax.sharding import PartitionSpec as P

MESH = pl.DeviceIdType.MESH
EPS = 1e-05
CH = 384
GROUP = 12
COLS = 64
F32 = jnp.float32
BF16 = jnp.bfloat16
UNITS = ((0, 1), (0, 0), (1, 1), (1, 0))


def dot(a, b):
    return jnp.dot(a, b, preferred_element_type=F32)


def exact_dot(a, onehot):
    high = a.astype(BF16)
    rest = a - high.astype(F32)
    middle = rest.astype(BF16)
    low = (rest - middle.astype(F32)).astype(BF16)
    parts = dot(jnp.concatenate([high.astype(F32), middle.astype(F32), low.astype(F32)], axis=0).astype(BF16), onehot)
    return parts[0:8] + parts[8:16] + parts[16:24]


def membership(shape, channel_axis):
    channel = lax.broadcasted_iota(jnp.int32, shape, channel_axis)
    first = lax.rem(lax.broadcasted_iota(jnp.int32, shape, 1 - channel_axis), 32) * GROUP
    return jnp.where((channel >= first) & (channel < first + GROUP), 1.0, 0.0).astype(BF16)


def kernel(
    cells, lat, counts, gain, nbias, w3, b3, w2, b2, out,
    x, act, wide, raw2, phase, acc, mid, pair, gath, inter, coef, ready, last,
    lsem, wsem, w2sem, p_s, p_r, g_s, g_r, z_s, z_r, h_s, h_r, c_s, c_r, m_s, m_r, o_s,
):
    n_t, n_s = lax.axis_size("tm"), lax.axis_size("space")
    t_me, s_me = lax.axis_index("tm"), lax.axis_index("space")
    later = {"tm": lax.rem(t_me + 1, n_t)}
    up, down = {"space": lax.rem(s_me + n_s - 1, n_s)}, {"space": lax.rem(s_me + 1, n_s)}

    def remote(src, dst, send, recv, device):
        return pltpu.make_async_remote_copy(
            src_ref=src, dst_ref=dst, send_sem=send, recv_sem=recv, device_id=device, device_id_type=MESH
        )

    own = pltpu.make_async_copy(lat, x.at[:, pl.ds(2, 2), pl.ds(2, 2)], lsem)
    own.start()

    column_peers = [{"tm": lax.rem(t_me + d, n_t)} for d in range(n_t)]
    row_peers = [{"space": lax.rem(s_me + d, n_s)} for d in range(n_s)]
    peers = column_peers[1:] + row_peers[1:]
    barrier = pltpu.get_barrier_semaphore()
    for peer in peers:
        pl.semaphore_signal(barrier, inc=1, device_id=peer, device_id_type=MESH)

    w2_copy = pltpu.make_async_copy(w2, raw2, w2sem)
    w2_copy.start()
    w3_copies = [
        pltpu.make_async_copy(w3.at[a, :, e], wide.at[a, :, :, pl.ds(e * CH, CH)], wsem.at[a * 3 + e])
        for a in (2, 1, 0)
        for e in range(3)
    ]
    for copy in w3_copies:
        copy.start()

    def present(c, frame):
        return (frame < counts[c]).astype(F32)

    own.wait()
    firsts, seconds = [], []
    for c in range(2):
        first = jnp.zeros((8, CH), F32)
        second = jnp.zeros((8, CH), F32)
        for f in range(2):
            f1 = jnp.zeros((8, CH), F32)
            f2 = jnp.zeros((8, CH), F32)
            for r in range(2):
                v = x[c, 2 + f, 2 + r].astype(F32).reshape(8, 8, CH)
                f1 += jnp.sum(v, axis=0)
                f2 += jnp.sum(v * v, axis=0)
            there = present(c, 2 * t_me + f)
            first += f1 * there
            second += f2 * there
        firsts.append(jnp.sum(first, axis=0, keepdims=True))
        seconds.append(jnp.sum(second, axis=0, keepdims=True))
    sums = jnp.concatenate(firsts + seconds + [jnp.zeros((4, CH), F32)], axis=0)
    grouped = exact_dot(sums, membership((CH, 128), 0))
    lane_row = lax.broadcasted_iota(jnp.int32, (8, 128), 1) // 32
    diagonal = lane_row == lax.broadcasted_iota(jnp.int32, (8, 128), 0)
    gath[0] = jnp.sum(jnp.where(diagonal, grouped, 0.0), axis=0, keepdims=True)

    pl.semaphore_wait(barrier, len(peers))

    sums_a = [remote(gath.at[0], gath.at[d], g_s.at[d], g_r.at[d], column_peers[d]) for d in range(1, n_t)]
    for copy in sums_a:
        copy.start()
    z_copies = {
        (c, f): remote(lat.at[c, f], x.at[c, f, pl.ds(2, 2)], z_s.at[c * 2 + f], z_r.at[c * 2 + f], later)
        for c, f in UNITS
    }

    @pl.when(t_me < n_t - 1)
    def _():
        for unit in UNITS:
            z_copies[unit].start()

    halo = []
    for c in range(2):
        halo.append((
            remote(lat.at[c, :, 1], x.at[c, pl.ds(2, 2), 1], h_s.at[2 * c], h_r.at[2 * c], down),
            remote(lat.at[c, :, 0], x.at[c, pl.ds(2, 2), 4], h_s.at[2 * c + 1], h_r.at[2 * c + 1], up),
        ))
    halo[1] += (
        remote(lat.at[1, 0, 0], x.at[1, 2, 0], h_s.at[4], h_r.at[4], down),
        remote(lat.at[1, 0, 1], x.at[1, 2, 5], h_s.at[5], h_r.at[5], up),
    )
    for both in halo:
        for copy in both:
            copy.start()

    def fold(i, carry):
        rows = pl.ds(pl.multiple_of(i * 64, 64), 64)
        by_row = [[raw2[b, e, rows].astype(F32) for e in range(3)] for b in range(3)]
        for p, u, picks in ((0, 0, (0,)), (0, 1, (1, 2)), (1, 0, (0, 1)), (1, 1, (2,))):
            taps = [functools.reduce(jnp.add, [by_row[b][e] for b in picks]) for e in range(3)]
            phase[p, u, rows, 0:CH] = taps[0].astype(BF16)
            phase[p, u, rows, CH : 2 * CH] = (taps[0] + taps[1] + taps[2]).astype(BF16)
            phase[p, u, rows, 2 * CH : 3 * CH] = taps[2].astype(BF16)
        return carry

    for copy in sums_a:
        copy.wait_recv()
    part = gath[0]
    for d in range(1, n_t):
        part = part + gath[d]
    pair[0] = part
    sums_b = [remote(pair.at[0], pair.at[d], p_s.at[d], p_r.at[d], row_peers[d]) for d in range(1, n_s)]
    for copy in sums_b:
        copy.start()

    w2_copy.wait()
    lax.fori_loop(0, CH // 64, fold, 0)

    corner = {}
    for c, f in UNITS:
        slot = c * 4 + f * 2
        if c == 0:
            rows = ((x.at[c, f, 3], x.at[c, f, 1]), (x.at[c, f, 2], x.at[c, f, 4]))
        else:
            rows = tuple((x.at[c, f, pl.ds(2, 2)], x.at[c, f, pl.ds(start, 2)]) for start in (0, 4))
        corner[c, f] = (
            remote(*rows[0], c_s.at[slot], c_r.at[slot], down),
            remote(*rows[1], c_s.at[slot + 1], c_r.at[slot + 1], up),
        )

    def forward(unit):
        @pl.when(t_me > 0)
        def _():
            z_copies[unit].wait_recv()
            for copy in corner[unit]:
                copy.start()

    forward(UNITS[0])

    for copy in sums_b:
        copy.wait_recv()
    total = pair[0]
    for d in range(1, n_s):
        total = total + pair[d]
    lane = lax.broadcasted_iota(jnp.int32, (1, 128), 1)
    second_clip = lax.rem(lane // 32, 2) == 1
    number = [(counts[c] * (cells * GROUP)).astype(F32) for c in range(2)]
    ratio = total / jnp.where(second_clip, number[1], number[0])
    mean = pltpu.roll(ratio, 64, 1)
    packed = jnp.where(lane < 64, ratio, lax.rsqrt(jnp.where(lane < 64, 0.0, ratio - mean * mean) + EPS))
    coef[...] = exact_dot(jnp.where(diagonal, packed, 0.0), membership((128, CH), 1))

    def activate(c, f, first=1, end=5):
        there = present(c, 2 * t_me - 2 + f)

        def row(r, carry):
            inside = jnp.where(((r < 2) & (s_me == 0)) | ((r > 3) & (s_me == n_s - 1)), 0.0, there)
            half = (x[c, f, r].astype(F32) - coef[c : c + 1]) * (coef[2 + c : 3 + c] * gain[...].reshape(1, CH) * 0.5) + nbias[...].reshape(1, CH) * 0.5
            act[c, f, r] = ((half + half * jnp.tanh(half)) * inside).astype(BF16)
            return carry

        lax.fori_loop(first, end, row, 0)

    def column(v):
        return lax.rem(lax.broadcasted_iota(jnp.int32, v.shape, 0), COLS)

    def before(v):
        return jnp.where(column(v) > 0, pltpu.roll(v, 1, 0), 0.0)

    def after(v):
        return jnp.where(column(v) < COLS - 1, pltpu.roll(v, v.shape[0] - 1, 0), 0.0)

    OWN, WIDE = (2, 3), (1, 2, 3, 4)

    def volume(c, frames, taps, rows=OWN):
        lhs = jnp.concatenate(
            [jnp.concatenate([act[c, f, r - 1 + b] for f in frames for b in range(3)], axis=1) for r in rows], axis=0
        )
        rhs = wide[pl.ds(taps[0], len(taps))].reshape(len(taps) * 3 * CH, 3 * CH)
        prod = dot(lhs, rhs)
        return before(prod[:, 0:CH]) + prod[:, CH : 2 * CH] + after(prod[:, 2 * CH :])

    def finish(c, f, rows=OWN):
        kept = present(c, 2 * t_me + f)
        resid = jnp.concatenate([x[c, 2 + f, r] for r in rows], axis=0).astype(F32)
        sums = last[...] if rows is WIDE else acc[c, f]
        value = ((resid + sums + b3[...].reshape(1, CH)) * kept).astype(BF16)
        for i, r in enumerate(rows):
            mid[c, f, r - 1] = value[i * COLS : (i + 1) * COLS]

    mid_copies = [
        (
            remote(mid.at[0, :, 2], mid.at[0, :, 0], m_s.at[0], m_r.at[0], down),
            remote(mid.at[0, :, 1], mid.at[0, :, 3], m_s.at[1], m_r.at[1], up),
        ),
        (
            remote(mid.at[1, 1, 2], mid.at[1, 1, 0], m_s.at[2], m_r.at[2], down),
            remote(mid.at[1, 1, 1], mid.at[1, 1, 3], m_s.at[3], m_r.at[3], up),
        ),
    ]

    stored = [
        pltpu.make_async_copy(ready.at[i // 4, :, i % 4], out.at[i // 4, :, i % 4], o_s.at[i]) for i in range(8)
    ]

    def emit(c, p, r, first_row):
        lhs = jnp.concatenate([jnp.concatenate([mid[c, f, first_row], mid[c, f, first_row + 1]], axis=1) for f in range(2)], axis=0)
        prod = dot(lhs, phase[p].reshape(2 * CH, 3 * CH))
        left, centre, right = prod[:, 0:CH], prod[:, CH : 2 * CH], prod[:, 2 * CH :]
        centre = centre + b2[...].reshape(1, CH)
        even = centre + (before(left) - left)
        odd = centre + (after(right) - right)
        for f in range(2):
            kept = present(c, 2 * t_me + f)
            for lane in range(CH // 128):
                cut = slice(lane * 128, lane * 128 + 128)
                rows = slice(f * COLS, (f + 1) * COLS)
                inter[f, lane, pl.ds(0, COLS, stride=2)] = even[rows, cut] * kept
                inter[f, lane, pl.ds(1, COLS, stride=2)] = odd[rows, cut] * kept
                ready[c, f, 2 * r + p, :, cut] = inter[f, lane].astype(BF16)
        stored[c * 4 + 2 * r + p].start()

    def inner(c):
        emit(c, 1, 0, 1)
        emit(c, 0, 1, 1)

    def outer(c):
        for copy in mid_copies[c]:
            copy.wait_recv()

        @pl.when(s_me == 0)
        def _():
            mid[c, :, 0] = jnp.zeros((2, COLS, CH), BF16)

        @pl.when(s_me == n_s - 1)
        def _():
            mid[c, :, 3] = jnp.zeros((2, COLS, CH), BF16)

        emit(c, 0, 0, 0)
        emit(c, 1, 1, 2)

    def arrived(unit):
        for copy in corner[unit]:
            copy.wait_recv()

    for copy in halo[0]:
        copy.wait_recv()
    activate(0, 2)
    activate(0, 3)
    forward(UNITS[1])
    for copy in w3_copies:
        copy.wait()
    acc[0, 0] = volume(0, (2,), (2,))
    acc[0, 1] = volume(0, (2, 3), (1, 2))
    for copy in halo[1]:
        copy.wait_recv()
    activate(1, 2, 0, 6)
    activate(1, 3)
    forward(UNITS[2])
    last[...] = volume(1, (2,), (2,), WIDE)
    acc[1, 1] = volume(1, (2, 3), (1, 2))
    forward(UNITS[3])

    @pl.when(t_me > 0)
    def _():
        arrived((0, 1))
        activate(0, 1)
        arrived((0, 0))
        activate(0, 0)
        acc[0, 1] += volume(0, (1,), (0,))
        acc[0, 0] += volume(0, (0, 1), (0, 1))

    finish(0, 0)
    finish(0, 1)
    for copy in mid_copies[0]:
        copy.start()

    @pl.when(t_me > 0)
    def _():
        arrived((1, 1))
        activate(1, 1, 0, 6)
        acc[1, 1] += volume(1, (1,), (0,))

    finish(1, 1)
    for copy in mid_copies[1]:
        copy.start()

    @pl.when(t_me > 0)
    def _():
        last[...] += volume(1, (1,), (1,), WIDE)

    inner(0)

    @pl.when(t_me > 0)
    def _():
        arrived((1, 0))
        activate(1, 0, 0, 6)
        last[...] += volume(1, (0,), (0,), WIDE)

    finish(1, 0, WIDE)
    outer(0)
    inner(1)
    outer(1)

    for copy in stored:
        copy.wait()

    for copy in sums_a + sums_b + [copy for both in halo + mid_copies for copy in both]:
        copy.wait_send()

    @pl.when(t_me < n_t - 1)
    def _():
        for unit in UNITS:
            z_copies[unit].wait_send()

    @pl.when(t_me > 0)
    def _():
        for unit in UNITS:
            for copy in corner[unit]:
                copy.wait_send()


def pass_on(given, out, held, i_s, o_s):
    part = lambda ref, i: ref.at[i // 4, i // 2 % 2, pl.ds(i % 2 * 2, 2)]
    loads = [pltpu.make_async_copy(part(given, i), part(held, i), i_s.at[i]) for i in range(8)]
    stores = [pltpu.make_async_copy(part(held, i), part(out, i), o_s.at[i]) for i in range(8)]
    for load in loads:
        load.start()
    for load, store in zip(loads, stores):
        load.wait()
        store.start()
    for store in stores:
        store.wait()


def body(latents, frame_counts, norm_gain, norm_bias, conv3_weight, conv3_bias, conv2_weight, conv2_bias):
    rows = latents.shape[2] * lax.axis_size("space")
    hbm, vmem, smem = (pl.BlockSpec(memory_space=space) for space in (pltpu.HBM, pltpu.VMEM, pltpu.SMEM))
    dma = pltpu.SemaphoreType.DMA
    decoded = pl.pallas_call(
        functools.partial(kernel, rows * COLS),
        out_shape=jax.ShapeDtypeStruct((2, 2, 4, 2 * COLS, CH), BF16),
        in_specs=[hbm, smem, vmem, vmem, hbm, vmem, hbm, vmem],
        out_specs=hbm,
        scratch_shapes=[
            pltpu.VMEM((2, 4, 6, COLS, CH), BF16),
            pltpu.VMEM((2, 4, 6, COLS, CH), BF16),
            pltpu.VMEM((3, 3, CH, 3 * CH), BF16),
            pltpu.VMEM((3, 3, CH, CH), BF16),
            pltpu.VMEM((2, 2, CH, 3 * CH), BF16),
            pltpu.VMEM((2, 2, 2 * COLS, CH), F32),
            pltpu.VMEM((2, 2, 4, COLS, CH), BF16),
            pltpu.VMEM((8, 1, 128), F32),
            pltpu.VMEM((4, 1, 128), F32),
            pltpu.VMEM((2, 3, 2 * COLS, 128), F32),
            pltpu.VMEM((8, CH), F32),
            pltpu.VMEM((2, 2, 4, 2 * COLS, CH), BF16),
            pltpu.VMEM((4 * COLS, CH), F32),
            dma, dma((9,)), dma, dma((8,)), dma((8,)), dma((4,)), dma((4,)),
            dma((4,)), dma((4,)), dma((8,)), dma((8,)), dma((8,)), dma((8,)), dma((4,)), dma((4,)), dma((8,)),
        ],
        compiler_params=pltpu.CompilerParams(collective_id=0, has_side_effects=True, vmem_limit_bytes=58 * 2**20),
        cost_estimate=pl.CostEstimate(flops=7 * 10**9, bytes_accessed=13 * 10**6, transcendentals=10**6),
    )(latents, frame_counts, norm_gain, norm_bias, conv3_weight, conv3_bias, conv2_weight, conv2_bias)
    return pl.pallas_call(
        pass_on,
        out_shape=jax.ShapeDtypeStruct(decoded.shape, BF16),
        in_specs=[hbm],
        out_specs=hbm,
        scratch_shapes=[pltpu.VMEM(decoded.shape, BF16), dma((8,)), dma((8,))],
        compiler_params=pltpu.CompilerParams(vmem_limit_bytes=58 * 2**20),
    )(decoded)


def solution(mesh):
    placed = (P("clip", "tm", "space", None, None), P("clip"), P(), P(), P(), P(), P(), P())
    return jax.shard_map(
        body, mesh=mesh, in_specs=placed, out_specs=P("clip", "tm", "space", None, None), check_vma=False
    )
```

time: 28.6 us -> 27.4 us (0.958)
  local copies, waits for them, and re-layouts: 2.76 us -> 0 us
  Pallas kernels: 25.7 us -> 27.2 us
    unnamed x1 -> x0, local copies, waits for them, and re-layouts: 2.76 us -> none
    pallas_call x0 -> x1, Pallas kernels: none -> 2.29 us  [body(): pl.pallas_call(pass_on, out_shape=jax.ShapeDtypeStruct(decoded.shape, BF1...]
    pallas_call x1, Pallas kernels: 25.7 us -> 24.9 us  [body(): pl.pallas_call(functools.partial(kernel, rows * COLS), out_shape=jax.Shap...]
where the time goes in v2:
time: 27.4 us; the launch traced here: 27.2 us
  Pallas kernels  27.2 us (99%)
    pallas_call x1, Pallas kernels, body(): pl.pallas_call(functools.partial(kernel, rows * COLS), out_shape=jax.Shap...  24.9 us
    pallas_call x1, Pallas kernels, body(): pl.pallas_call(pass_on, out_shape=jax.ShapeDtypeStruct(decoded.shape, BF1...  2.29 us

profile of v2, /device:TPU:40, one launch (start us, length us, event | category | flops | bytes accessed | tf_op | source)
XLA Modules:
  0.0 27.2 jit_solution(13780812192949044649)
XLA Ops:
  0.0 24.9 %shard_map.82.given = bf16[2,2,4,128,384]{4,3,2,1,0:T(8,128)(2,1)} custom-call(bf16[2,2,2,64,384]{4,3,2,1,0:T(8,128)(2,1)} %lat.1, s32[2]{0:T(128)} %counts.1, f32[384]{0:T(512)} %gain.1, f32[384]{0:T(512)} %nbias.1, bf16[3,3,3,384,384]{4,3,2,1,0:T(8,128)(2,1)} %w3.1, f32[384]{0:T(512)} %b3.1, bf16[3,3,384,384]{3,2,1,0:T(8,128)(2,1)} %w2.1, f32[384]{0:T(512)} %b2.1), custom_call_target="tpu_custom_call" | custom-call | flops 7000000000 | bytes 13000000 | tf_op jit(solution)/shard_map/pallas_call | solution.py:373
  24.9 2.3 %shard_map.83 = bf16[2,2,4,128,384]{4,3,2,1,0:T(8,128)(2,1)} custom-call(bf16[2,2,4,128,384]{4,3,2,1,0:T(8,128)(2,1)} %shard_map.82.given), custom_call_target="tpu_custom_call" | custom-call | tf_op jit(solution)/shard_map/pallas_call | solution.py:398

commit v3 on v2

--- a/solution.py
+++ b/solution.py
@@ -205,9 +205,14 @@
 
     OWN, WIDE = (2, 3), (1, 2, 3, 4)
 
-    def volume(c, frames, taps, rows=OWN):
+    def volume(parts, taps):
         lhs = jnp.concatenate(
-            [jnp.concatenate([act[c, f, r - 1 + b] for f in frames for b in range(3)], axis=1) for r in rows], axis=0
+            [
+                jnp.concatenate([act[c, f, r - 1 + b] for f in frames for b in range(3)], axis=1)
+                for c, frames, rows in parts
+                for r in rows
+            ],
+            axis=0,
         )
         rhs = wide[pl.ds(taps[0], len(taps))].reshape(len(taps) * 3 * CH, 3 * CH)
         prod = dot(lhs, rhs)
@@ -236,28 +241,32 @@
         pltpu.make_async_copy(ready.at[i // 4, :, i % 4], out.at[i // 4, :, i % 4], o_s.at[i]) for i in range(8)
     ]
 
-    def emit(c, p, r, first_row):
-        lhs = jnp.concatenate([jnp.concatenate([mid[c, f, first_row], mid[c, f, first_row + 1]], axis=1) for f in range(2)], axis=0)
+    def emit(c, p, picks=(0, 1)):
+        lhs = jnp.concatenate(
+            [
+                jnp.concatenate([mid[c, f, r + p], mid[c, f, r + p + 1]], axis=1)
+                for r in picks
+                for f in range(2)
+            ],
+            axis=0,
+        )
         prod = dot(lhs, phase[p].reshape(2 * CH, 3 * CH))
         left, centre, right = prod[:, 0:CH], prod[:, CH : 2 * CH], prod[:, 2 * CH :]
         centre = centre + b2[...].reshape(1, CH)
         even = centre + (before(left) - left)
         odd = centre + (after(right) - right)
-        for f in range(2):
-            kept = present(c, 2 * t_me + f)
-            for lane in range(CH // 128):
-                cut = slice(lane * 128, lane * 128 + 128)
-                rows = slice(f * COLS, (f + 1) * COLS)
-                inter[f, lane, pl.ds(0, COLS, stride=2)] = even[rows, cut] * kept
-                inter[f, lane, pl.ds(1, COLS, stride=2)] = odd[rows, cut] * kept
-                ready[c, f, 2 * r + p, :, cut] = inter[f, lane].astype(BF16)
-        stored[c * 4 + 2 * r + p].start()
-
-    def inner(c):
-        emit(c, 1, 0, 1)
-        emit(c, 0, 1, 1)
-
-    def outer(c):
+        for i, r in enumerate(picks):
+            for f in range(2):
+                kept = present(c, 2 * t_me + f)
+                rows = slice((2 * i + f) * COLS, (2 * i + f + 1) * COLS)
+                for lane in range(CH // 128):
+                    cut = slice(lane * 128, lane * 128 + 128)
+                    inter[f, lane, pl.ds(0, COLS, stride=2)] = even[rows, cut] * kept
+                    inter[f, lane, pl.ds(1, COLS, stride=2)] = odd[rows, cut] * kept
+                    ready[c, f, 2 * r + p, :, cut] = inter[f, lane].astype(BF16)
+            stored[c * 4 + 2 * r + p].start()
+
+    def decode(c):
         for copy in mid_copies[c]:
             copy.wait_recv()
 
@@ -269,29 +278,34 @@
         def _():
             mid[c, :, 3] = jnp.zeros((2, COLS, CH), BF16)
 
-        emit(c, 0, 0, 0)
-        emit(c, 1, 1, 2)
+        if c == 0:
+            emit(c, 0, (0,))
+            emit(c, 1, (1,))
+        else:
+            emit(c, 0)
+            emit(c, 1)
 
     def arrived(unit):
         for copy in corner[unit]:
             copy.wait_recv()
 
-    for copy in halo[0]:
-        copy.wait_recv()
+    for both in halo:
+        for copy in both:
+            copy.wait_recv()
     activate(0, 2)
     activate(0, 3)
     forward(UNITS[1])
+    activate(1, 2, 0, 6)
+    activate(1, 3)
     for copy in w3_copies:
         copy.wait()
-    acc[0, 0] = volume(0, (2,), (2,))
-    acc[0, 1] = volume(0, (2, 3), (1, 2))
-    for copy in halo[1]:
-        copy.wait_recv()
-    activate(1, 2, 0, 6)
-    activate(1, 3)
+    value = volume(((0, (2, 3), OWN), (1, (2, 3), OWN)), (1, 2))
+    acc[0, 1] = value[: 2 * COLS]
+    acc[1, 1] = value[2 * COLS :]
     forward(UNITS[2])
-    last[...] = volume(1, (2,), (2,), WIDE)
-    acc[1, 1] = volume(1, (2, 3), (1, 2))
+    value = volume(((0, (2,), OWN), (1, (2,), WIDE)), (2,))
+    acc[0, 0] = value[: 2 * COLS]
+    last[...] = value[2 * COLS :]
     forward(UNITS[3])
 
     @pl.when(t_me > 0)
@@ -300,8 +314,8 @@
         activate(0, 1)
         arrived((0, 0))
         activate(0, 0)
-        acc[0, 1] += volume(0, (1,), (0,))
-        acc[0, 0] += volume(0, (0, 1), (0, 1))
+        acc[0, 1] += volume(((0, (1,), OWN),), (0,))
+        acc[0, 0] += volume(((0, (0, 1), OWN),), (0, 1))
 
     finish(0, 0)
     finish(0, 1)
@@ -312,7 +326,7 @@
     def _():
         arrived((1, 1))
         activate(1, 1, 0, 6)
-        acc[1, 1] += volume(1, (1,), (0,))
+        acc[1, 1] += volume(((1, (1,), OWN),), (0,))
 
     finish(1, 1)
     for copy in mid_copies[1]:
@@ -320,20 +334,21 @@
 
     @pl.when(t_me > 0)
     def _():
-        last[...] += volume(1, (1,), (1,), WIDE)
-
-    inner(0)
+        last[...] += volume(((1, (1,), WIDE),), (1,))
+
+
+    emit(0, 1, (0,))
+    emit(0, 0, (1,))
 
     @pl.when(t_me > 0)
     def _():
         arrived((1, 0))
         activate(1, 0, 0, 6)
-        last[...] += volume(1, (0,), (0,), WIDE)
+        last[...] += volume(((1, (0,), WIDE),), (0,))
 
     finish(1, 0, WIDE)
-    outer(0)
-    inner(1)
-    outer(1)
+    decode(0)
+    decode(1)
 
     for copy in stored:
         copy.wait()
@@ -354,9 +369,9 @@
 
 
 def pass_on(given, out, held, i_s, o_s):
-    part = lambda ref, i: ref.at[i // 4, i // 2 % 2, pl.ds(i % 2 * 2, 2)]
-    loads = [pltpu.make_async_copy(part(given, i), part(held, i), i_s.at[i]) for i in range(8)]
-    stores = [pltpu.make_async_copy(part(held, i), part(out, i), o_s.at[i]) for i in range(8)]
+    part = lambda ref, i: ref.at[i // 2, i % 2]
+    loads = [pltpu.make_async_copy(part(given, i), part(held, i), i_s.at[i]) for i in range(4)]
+    stores = [pltpu.make_async_copy(part(held, i), part(out, i), o_s.at[i]) for i in range(4)]
     for load in loads:
         load.start()
     for load, store in zip(loads, stores):
@@ -400,7 +415,7 @@
         out_shape=jax.ShapeDtypeStruct(decoded.shape, BF16),
         in_specs=[hbm],
         out_specs=hbm,
-        scratch_shapes=[pltpu.VMEM(decoded.shape, BF16), dma((8,)), dma((8,))],
+        scratch_shapes=[pltpu.VMEM(decoded.shape, BF16), dma((4,)), dma((4,))],
         compiler_params=pltpu.CompilerParams(vmem_limit_bytes=58 * 2**20),
     )(decoded)
 

time: 27.4 us -> 27.6 us (level)
  Pallas kernels: 27.2 us -> 27.5 us
    pallas_call x1, Pallas kernels: 24.9 us -> 25.3 us  [body(): pl.pallas_call(functools.partial(kernel, rows * COLS), out_shape=jax.Shap...]
where the time goes in v3:
time: 27.6 us; the launch traced here: 27.5 us
  Pallas kernels  27.5 us (100%)
    pallas_call x1, Pallas kernels, body(): pl.pallas_call(functools.partial(kernel, rows * COLS), out_shape=jax.Shap...  25.3 us
    pallas_call x1, Pallas kernels, body(): pl.pallas_call(pass_on, out_shape=jax.ShapeDtypeStruct(decoded.shape, BF1...  2.2 us

profile of v3, /device:TPU:40, one launch (start us, length us, event | category | flops | bytes accessed | tf_op | source)
XLA Modules:
  0.0 27.5 jit_solution(10695811256506697204)
XLA Ops:
  0.0 25.3 %shard_map.82.given = bf16[2,2,4,128,384]{4,3,2,1,0:T(8,128)(2,1)} custom-call(bf16[2,2,2,64,384]{4,3,2,1,0:T(8,128)(2,1)} %lat.1, s32[2]{0:T(128)} %counts.1, f32[384]{0:T(512)} %gain.1, f32[384]{0:T(512)} %nbias.1, bf16[3,3,3,384,384]{4,3,2,1,0:T(8,128)(2,1)} %w3.1, f32[384]{0:T(512)} %b3.1, bf16[3,3,384,384]{3,2,1,0:T(8,128)(2,1)} %w2.1, f32[384]{0:T(512)} %b2.1), custom_call_target="tpu_custom_call" | custom-call | flops 7000000000 | bytes 13000000 | tf_op jit(solution)/shard_map/pallas_call | solution.py:388
  25.3 2.2 %shard_map.83 = bf16[2,2,4,128,384]{4,3,2,1,0:T(8,128)(2,1)} custom-call(bf16[2,2,4,128,384]{4,3,2,1,0:T(8,128)(2,1)} %shard_map.82.given), custom_call_target="tpu_custom_call" | custom-call | tf_op jit(solution)/shard_map/pallas_call | solution.py:413

commit v4 on v2

--- a/solution.py
+++ b/solution.py
@@ -354,9 +354,9 @@
 
 
 def pass_on(given, out, held, i_s, o_s):
-    part = lambda ref, i: ref.at[i // 4, i // 2 % 2, pl.ds(i % 2 * 2, 2)]
-    loads = [pltpu.make_async_copy(part(given, i), part(held, i), i_s.at[i]) for i in range(8)]
-    stores = [pltpu.make_async_copy(part(held, i), part(out, i), o_s.at[i]) for i in range(8)]
+    part = lambda ref, i: ref.at[i // 2, i % 2]
+    loads = [pltpu.make_async_copy(part(given, i), part(held, i), i_s.at[i]) for i in range(4)]
+    stores = [pltpu.make_async_copy(part(held, i), part(out, i), o_s.at[i]) for i in range(4)]
     for load in loads:
         load.start()
     for load, store in zip(loads, stores):
@@ -400,7 +400,7 @@
         out_shape=jax.ShapeDtypeStruct(decoded.shape, BF16),
         in_specs=[hbm],
         out_specs=hbm,
-        scratch_shapes=[pltpu.VMEM(decoded.shape, BF16), dma((8,)), dma((8,))],
+        scratch_shapes=[pltpu.VMEM(decoded.shape, BF16), dma((4,)), dma((4,))],
         compiler_params=pltpu.CompilerParams(vmem_limit_bytes=58 * 2**20),
     )(decoded)
 

time: 27.4 us -> 27.3 us (level)
  no operation moved by 1% of the time
where the time goes in v4:
time: 27.3 us; the launch traced here: 27.1 us
  Pallas kernels  27.1 us (99%)
    pallas_call x1, Pallas kernels, body(): pl.pallas_call(functools.partial(kernel, rows * COLS), out_shape=jax.Shap...  24.9 us
    pallas_call x1, Pallas kernels, body(): pl.pallas_call(pass_on, out_shape=jax.ShapeDtypeStruct(decoded.shape, BF1...  2.2 us

profile of v4, /device:TPU:40, one launch (start us, length us, event | category | flops | bytes accessed | tf_op | source)
XLA Modules:
  0.0 27.1 jit_solution(5107201522977549310)
XLA Ops:
  0.0 24.9 %shard_map.82.given = bf16[2,2,4,128,384]{4,3,2,1,0:T(8,128)(2,1)} custom-call(bf16[2,2,2,64,384]{4,3,2,1,0:T(8,128)(2,1)} %lat.1, s32[2]{0:T(128)} %counts.1, f32[384]{0:T(512)} %gain.1, f32[384]{0:T(512)} %nbias.1, bf16[3,3,3,384,384]{4,3,2,1,0:T(8,128)(2,1)} %w3.1, f32[384]{0:T(512)} %b3.1, bf16[3,3,384,384]{3,2,1,0:T(8,128)(2,1)} %w2.1, f32[384]{0:T(512)} %b2.1), custom_call_target="tpu_custom_call" | custom-call | flops 7000000000 | bytes 13000000 | tf_op jit(solution)/shard_map/pallas_call | solution.py:373
  24.9 2.2 %shard_map.83 = bf16[2,2,4,128,384]{4,3,2,1,0:T(8,128)(2,1)} custom-call(bf16[2,2,4,128,384]{4,3,2,1,0:T(8,128)(2,1)} %shard_map.82.given), custom_call_target="tpu_custom_call" | custom-call | tf_op jit(solution)/shard_map/pallas_call | solution.py:398
